TPU v7x, 32 devices: a whole 2x2x4 slice. The times are simulated.
32 devices in a mesh: grp: 4 (over x, core), box: 8 (over z, y).
Axes of the slice: x: 2, y: 2, z: 4, core: 2. Of those that a mesh axis runs over, the one named last changes fastest.
Arguments:
- right_side: float32 [64, 256, 128], P('grp', 'box'), may hold values from -6 to 6
- beta: float32 [64, 256, 128], P('grp', 'box'), may hold values from 0.25 to 4
Outputs:
- correction: float32 [64, 256, 128], P('grp', 'box')
All inputs are finite; a program needn't handle non-finite values.
Results may differ from a plain program's by a relative error of at most 0.0001.
Values sent between devices are 32-bit elements; how exact they have to be, the bound alone decides.
A program may use at most 64 MiB of HBM per device.

v0:
```python
import jax
import jax.numpy as jnp
from jax import lax
from jax.sharding import PartitionSpec as P

LEVELS = 4
SWEEPS = 2
COARSE = 8


relax_weight = 2.0 / 3.0


def with_halo(shard, sides, width):
    for axis, dim in sides:
        size, length = (lax.axis_size(axis), shard.shape[dim])
        up = [(i, (i + 1) % size) for i in range(size - 1)]
        down = [(j, i) for i, j in up]
        last = lax.slice_in_dim(shard, length - width, length, axis=dim)
        leading = lax.slice_in_dim(shard, 0, width, axis=dim)
        before = lax.ppermute(last, axis, up)
        after = lax.ppermute(leading, axis, down)
        shard = jnp.concatenate([before, shard, after], axis=dim)
    return shard


def from_partner(block, axis, apart):
    count = lax.axis_size(axis)
    route = []
    for low in range(count):
        high = low | 1 << apart
        if high != low and high < count:
            route += [(low, high), (high, low)]
    return lax.ppermute(block, axis, route)


def pad_zeros(field):
    return jnp.pad(field, 1)


def pad_local(field):
    extended = with_halo(field, (("grp", 0), ("box", 1)), 1)
    return jnp.pad(extended, ((0, 0), (0, 0), (1, 1)))


def face_coeffs(padded_beta):
    face_x = 0.5 * (padded_beta[1:, 1:-1, 1:-1] + padded_beta[:-1, 1:-1, 1:-1])
    face_y = 0.5 * (padded_beta[1:-1, 1:, 1:-1] + padded_beta[1:-1, :-1, 1:-1])
    face_z = 0.5 * (padded_beta[1:-1, 1:-1, 1:] + padded_beta[1:-1, 1:-1, :-1])
    return (face_x, face_y, face_z)


def inverse_diagonal(coeffs, scale):
    face_x, face_y, face_z = coeffs
    total = (
        face_x[:-1]
        + face_x[1:]
        + face_y[:, :-1]
        + face_y[:, 1:]
        + face_z[:, :, :-1]
        + face_z[:, :, 1:]
    )
    return 1.0 / (scale * total)


def apply_operator(padded, coeffs, scale):
    face_x, face_y, face_z = coeffs
    centre = padded[1:-1, 1:-1, 1:-1]
    total = face_x[:-1] * (centre - padded[:-2, 1:-1, 1:-1]) + face_x[1:] * (
        centre - padded[2:, 1:-1, 1:-1]
    )
    total = (
        total
        + face_y[:, :-1] * (centre - padded[1:-1, :-2, 1:-1])
        + face_y[:, 1:] * (centre - padded[1:-1, 2:, 1:-1])
    )
    total = (
        total
        + face_z[:, :, :-1] * (centre - padded[1:-1, 1:-1, :-2])
        + face_z[:, :, 1:] * (centre - padded[1:-1, 1:-1, 2:])
    )
    return scale * total


def jacobi_sweeps(field, source, coeffs, inverse, scale, count, padder):
    for sweep_index in range(count):
        field = (
            field + relax_weight * (source - apply_operator(padder(field), coeffs, scale)) * inverse
        )
    return field


def conjugate_solve(source, coeffs, scale, count):
    field = jnp.zeros_like(source)
    remain = source
    direction = source
    norm_now = jnp.sum(remain * remain)
    for step_index in range(count):
        image = apply_operator(pad_zeros(direction), coeffs, scale)
        alpha = norm_now / jnp.sum(direction * image)
        field = field + alpha * direction
        remain = remain - alpha * image
        norm_next = jnp.sum(remain * remain)
        direction = remain + norm_next / norm_now * direction
        norm_now = norm_next
    return field


def restrict_mean(field):
    size_a, size_b, size_c = field.shape
    blocks = field.reshape(size_a // 2, 2, size_b // 2, 2, size_c // 2, 2)
    return jnp.mean(blocks, axis=(1, 3, 5))


def prolong_copy(field):
    return jnp.repeat(jnp.repeat(jnp.repeat(field, 2, axis=0), 2, axis=1), 2, axis=2)


def merge_groups(pieces):
    group_index = lax.axis_index("grp")
    for bit_index in range(lax.axis_size("grp").bit_length() - 1):
        partner = from_partner(pieces, "grp", bit_index)
        upper = group_index >> bit_index & 1 == 1
        pieces = tuple(
            (
                jnp.where(
                    upper,
                    jnp.concatenate([theirs, own_piece], 0),
                    jnp.concatenate([own_piece, theirs], 0),
                )
                for own_piece, theirs in zip(pieces, partner)
            )
        )
    return pieces


def merge_boxes(pieces):
    return lax.all_gather(pieces, "box", axis=1, tiled=True)


def shards(right_side, beta):
    source = right_side
    level_beta = beta
    saved = []
    for level in range(LEVELS):
        scale = 0.25**level
        coeffs = face_coeffs(pad_local(level_beta))
        inverse = inverse_diagonal(coeffs, scale)
        field = relax_weight * source * inverse
        field = jacobi_sweeps(field, source, coeffs, inverse, scale, SWEEPS - 1, pad_local)
        residual = source - apply_operator(pad_local(field), coeffs, scale)
        saved.append((field, source, coeffs, inverse, scale))
        source = restrict_mean(residual)
        level_beta = restrict_mean(level_beta)
    low_scale = 0.25**LEVELS
    whole_source, whole_beta = merge_boxes(merge_groups((source, level_beta)))
    low_coeffs = face_coeffs(pad_zeros(whole_beta))
    whole_field = conjugate_solve(whole_source, low_coeffs, low_scale, COARSE)
    block_a, block_b, block_c = source.shape
    field = lax.dynamic_slice(
        whole_field,
        (lax.axis_index("grp") * block_a, lax.axis_index("box") * block_b, 0),
        (block_a, block_b, block_c),
    )
    for level in range(LEVELS - 1, -1, -1):
        kept, level_source, coeffs, inverse, scale = saved[level]
        field = kept + prolong_copy(field)
        field = jacobi_sweeps(field, level_source, coeffs, inverse, scale, SWEEPS, pad_local)
    return field


def solution(mesh):
    placed = (P("grp", "box", None), P("grp", "box", None))
    return jax.shard_map(
        shards, mesh=mesh, in_specs=placed, out_specs=P("grp", "box", None), check_vma=False
    )
```

profile of v0, /device:TPU:0, one launch (start us, length us, event | category | flops | bytes accessed | tf_op | source)
XLA Modules:
  0.0 474.9 jit_solution(11404322440915359178)
XLA Ops:
  4.5 18.8 %reshape.81 = f32[8,2,16,2,64,2]{5,4,3,2,1,0:T(8,128)} reshape(f32[16,32,128]{2,1,0:T(8,128)} %param.3) | data formatting | bytes 524288 | tf_op jit(solution)/shard_map/reshape | solution.py:111
  23.4 7.0 %reduce_sum.231 = f32[8,16,64]{2,1,0:T(8,128)S(1)} reduce(f32[8,2,16,2,64,2]{5,4,3,2,1,0:T(8,128)} %reshape.81, f32[]{:T(128)} %constant.20.clone.1), dimensions={1,3,5}, to_apply=%region_1.2 | reduce | flops 57344 | bytes 294916 | tf_op jit(solution)/shard_map/reduce_sum | solution.py:112
  35.7 6.4 %collective-permute-start.37 = (f32[1,4,16]{2,1,0:T(4,128)S(1)}, f32[1,4,16]{2,1,0:T(4,128)S(1)}, u32[]{:S(2)}, u32[]{:S(2)}) collective-permute-start(f32[1,4,16]{2,1,0:T(4,128)S(1)} %get-tuple-element.114), channel_id=1, source_target_pairs={{0,8},{8,16},{16,24},{1,9},{9,17},{17,25},{2,10},{10,18},{18,26},{... | collective-permute-start | bytes 776 | tf_op jit(solution)/shard_map/ppermute | solution.py:21
  44.2 4.3 collective-permute-start.25
  54.7 5.1 %collective-permute-start.39 = (f32[4,1,16]{2,1,0:T(1,128)}, f32[4,1,16]{2,1,0:T(1,128)}, u32[]{:S(2)}, u32[]{:S(2)}) collective-permute-start(f32[4,1,16]{2,1,0:T(1,128)} %get-tuple-element.102), channel_id=1, source_target_pairs={{0,1},{1,2},{2,3},{3,4},{4,5},{5,6},{6,7},{8,9},{9,10},{10,11},{11... | collective-permute-start | bytes 776 | tf_op jit(solution)/shard_map/ppermute | solution.py:21
  61.2 4.5 collective-permute-start.3
  73.8 4.7 collective-permute-start.15
  78.5 5.1 %collective-permute-start.6 = (f32[18,1,128]{2,1,0:T(1,128)S(1)}, f32[18,1,128]{2,1,0:T(1,128)S(1)}, u32[]{:S(2)}, u32[]{:S(2)}) collective-permute-start(f32[18,1,128]{2,1,0:T(1,128)S(1)} %get-tuple-element.37), channel_id=1, source_target_pairs={{0,1},{1,2},{2,3},{3,4},{4,5},{5,6},{6,7},{8,9},{9,10},{10,11},{11... | collective-permute-start | bytes 27656 | tf_op jit(solution)/shard_map/ppermute | solution.py:21
  98.5 4.8 %collective-permute-start.10 = (f32[18,1,128]{2,1,0:T(1,128)S(1)}, f32[18,1,128]{2,1,0:T(1,128)S(1)}, u32[]{:S(2)}, u32[]{:S(2)}) collective-permute-start(f32[18,1,128]{2,1,0:T(1,128)S(1)} %get-tuple-element.35), channel_id=1, source_target_pairs={{0,1},{1,2},{2,3},{3,4},{4,5},{5,6},{6,7},{8,9},{9,10},{10,11},{11... | collective-permute-start | bytes 27656 | tf_op jit(solution)/shard_map/ppermute | solution.py:21
  104.7 4.2 collective-permute-done.11
  110.5 18.1 %reshape.80 = f32[8,2,16,2,64,2]{5,4,3,2,1,0:T(8,128)} reshape(f32[16,32,128]{2,1,0:T(8,128)S(1)} %fusion.45) | data formatting | bytes 524288 | tf_op jit(solution)/shard_map/reshape | solution.py:111
  128.5 7.0 %reduce_sum.230 = f32[8,16,64]{2,1,0:T(8,128)S(1)} reduce(f32[8,2,16,2,64,2]{5,4,3,2,1,0:T(8,128)} %reshape.80, f32[]{:T(128)} %constant.20.clone.1), dimensions={1,3,5}, to_apply=%region_0.1 | reduce | flops 57344 | bytes 294916 | tf_op jit(solution)/shard_map/reduce_sum | solution.py:112
  159.3 4.5 collective-permute-done.21
  234.5 30.4 %all_gather.7 = f32[4,16,8]{2,0,1:T(4,128)S(1)} all-gather(f32[4,2,8]{2,0,1:T(4,128)S(1)} %copy.215), channel_id=1, replica_groups=mesh['grp'=4,'box'=8] {'box'}, dimensions={1}, use_global_device_ids=true | all-gather | bytes 2304 | tf_op jit(solution)/shard_map/all_gather | solution.py:138
  278.3 30.4 %all_gather.6 = f32[4,16,8]{2,0,1:T(4,128)S(1)} all-gather(f32[4,2,8]{2,0,1:T(4,128)S(1)} %copy.214), channel_id=1, replica_groups=mesh['grp'=4,'box'=8] {'box'}, dimensions={1}, use_global_device_ids=true | all-gather | bytes 2304 | tf_op jit(solution)/shard_map/all_gather | solution.py:138
  348.8 4.2 collective-permute-done.55
  380.5 4.2 collective-permute-done.63
  396.9 4.2 collective-permute-done.67
  410.2 4.6 collective-permute-start.70
  416.2 4.2 collective-permute-done.71
  427.6 4.8 %collective-permute-start.74 = (f32[10,1,64]{2,1,0:T(1,128)S(1)}, f32[10,1,64]{2,1,0:T(1,128)S(1)}, u32[]{:S(2)}, u32[]{:S(2)}) collective-permute-start(f32[10,1,64]{2,1,0:T(1,128)S(1)} %get-tuple-element.51), channel_id=1, source_target_pairs={{0,1},{1,2},{2,3},{3,4},{4,5},{5,6},{6,7},{8,9},{9,10},{10,11},{11... | collective-permute-start | bytes 7688 | tf_op jit(solution)/shard_map/ppermute | solution.py:21
  433.7 4.2 collective-permute-done.75
  452.1 4.2 collective-permute-done.79
  469.2 4.2 collective-permute-done.83
  (334 shorter events, 259.9 us)
Async XLA Ops:
  0.7 59.1 %collective-permute-start.1 = (f32[1,32,128]{2,1,0:T(8,128)S(1)}, f32[1,32,128]{2,1,0:T(8,128)S(1)}, u32[]{:S(2)}, u32[]{:S(2)}) collective-permute-start(f32[1,32,128]{2,1,0:T(8,128)S(1)} %get-tuple-element.50), channel_id=1, source_target_pairs={{0,8},{8,16},{16,24},{1,9},{9,17},{17,25},{2,10},{10,18},{18,26},{... | collective-permute-start | bytes 49160 | tf_op jit(solution)/shard_map/ppermute | solution.py:21
  3.1 56.8 %collective-permute-start = (f32[1,32,128]{2,1,0:T(8,128)S(1)}, f32[1,32,128]{2,1,0:T(8,128)S(1)}, u32[]{:S(2)}, u32[]{:S(2)}) collective-permute-start(f32[1,32,128]{2,1,0:T(8,128)S(1)} %get-tuple-element.49), channel_id=1, source_target_pairs={{8,0},{16,8},{24,16},{9,1},{17,9},{25,17},{10,2},{18,10},{26,18},{... | collective-permute-start | bytes 49160 | tf_op jit(solution)/shard_map/ppermute | solution.py:22
  30.4 23.0 %collective-permute-start.12 = (f32[1,16,64]{2,1,0:T(8,128)S(1)}, f32[1,16,64]{2,1,0:T(8,128)S(1)}, u32[]{:S(2)}, u32[]{:S(2)}) collective-permute-start(f32[1,16,64]{2,1,0:T(8,128)S(1)} %get-tuple-element.70), channel_id=1, source_target_pairs={{8,0},{16,8},{24,16},{9,1},{17,9},{25,17},{10,2},{18,10},{26,18},{... | collective-permute-start | bytes 12296 | tf_op jit(solution)/shard_map/ppermute | solution.py:22
  34.4 8.5 %collective-permute-start.36 = (f32[1,4,16]{2,1,0:T(4,128)S(1)}, f32[1,4,16]{2,1,0:T(4,128)S(1)}, u32[]{:S(2)}, u32[]{:S(2)}) collective-permute-start(f32[1,4,16]{2,1,0:T(4,128)S(1)} %get-tuple-element.115), channel_id=1, source_target_pairs={{8,0},{16,8},{24,16},{9,1},{17,9},{25,17},{10,2},{18,10},{26,18},{... | collective-permute-start | bytes 776 | tf_op jit(solution)/shard_map/ppermute | solution.py:22
  35.7 8.5 %collective-permute-start.37 = (f32[1,4,16]{2,1,0:T(4,128)S(1)}, f32[1,4,16]{2,1,0:T(4,128)S(1)}, u32[]{:S(2)}, u32[]{:S(2)}) collective-permute-start(f32[1,4,16]{2,1,0:T(4,128)S(1)} %get-tuple-element.114), channel_id=1, source_target_pairs={{0,8},{8,16},{16,24},{1,9},{9,17},{17,25},{2,10},{10,18},{18,26},{... | collective-permute-start | bytes 776 | tf_op jit(solution)/shard_map/ppermute | solution.py:21
  42.9 6.2 %collective-permute-start.24 = (f32[1,8,32]{2,1,0:T(8,128)S(1)}, f32[1,8,32]{2,1,0:T(8,128)S(1)}, u32[]{:S(2)}, u32[]{:S(2)}) collective-permute-start(f32[1,8,32]{2,1,0:T(8,128)S(1)} %get-tuple-element.93), channel_id=1, source_target_pairs={{8,0},{16,8},{24,16},{9,1},{17,9},{25,17},{10,2},{18,10},{26,18},{... | collective-permute-start | bytes 3080 | tf_op jit(solution)/shard_map/ppermute | solution.py:22
  44.2 8.5 %collective-permute-start.25 = (f32[1,8,32]{2,1,0:T(8,128)S(1)}, f32[1,8,32]{2,1,0:T(8,128)S(1)}, u32[]{:S(2)}, u32[]{:S(2)}) collective-permute-start(f32[1,8,32]{2,1,0:T(8,128)S(1)} %get-tuple-element.92), channel_id=1, source_target_pairs={{0,8},{8,16},{16,24},{1,9},{9,17},{17,25},{2,10},{10,18},{18,26},{... | collective-permute-start | bytes 3080 | tf_op jit(solution)/shard_map/ppermute | solution.py:21
  52.7 165.3 %collective-permute-start.50 = (f32[1,2,8]{2,1,0:T(2,128)}, f32[1,2,8]{2,1,0:T(2,128)}, u32[]{:S(2)}, u32[]{:S(2)}) collective-permute-start(f32[1,2,8]{2,1,0:T(2,128)} %multiply_bitcast_fusion), channel_id=1, source_target_pairs={{0,8},{8,0},{16,24},{24,16},{1,9},{9,1},{17,25},{25,17},{2,10},{10... | collective-permute-start | bytes 200 | tf_op jit(solution)/shard_map/ppermute | solution.py:34
  53.4 137.5 %collective-permute-start.38 = (f32[4,1,16]{2,1,0:T(1,128)}, f32[4,1,16]{2,1,0:T(1,128)}, u32[]{:S(2)}, u32[]{:S(2)}) collective-permute-start(f32[4,1,16]{2,1,0:T(1,128)} %get-tuple-element.103), channel_id=1, source_target_pairs={{1,0},{2,1},{3,2},{4,3},{5,4},{6,5},{7,6},{9,8},{10,9},{11,10},{12... | collective-permute-start | bytes 776 | tf_op jit(solution)/shard_map/ppermute | solution.py:22
  54.7 136.3 %collective-permute-start.39 = (f32[4,1,16]{2,1,0:T(1,128)}, f32[4,1,16]{2,1,0:T(1,128)}, u32[]{:S(2)}, u32[]{:S(2)}) collective-permute-start(f32[4,1,16]{2,1,0:T(1,128)} %get-tuple-element.102), channel_id=1, source_target_pairs={{0,1},{1,2},{2,3},{3,4},{4,5},{5,6},{6,7},{8,9},{9,10},{10,11},{11... | collective-permute-start | bytes 776 | tf_op jit(solution)/shard_map/ppermute | solution.py:21
  71.5 7.0 %collective-permute-start.14 = (f32[10,1,64]{2,1,0:T(1,128)S(1)}, f32[10,1,64]{2,1,0:T(1,128)S(1)}, u32[]{:S(2)}, u32[]{:S(2)}) collective-permute-start(f32[10,1,64]{2,1,0:T(1,128)S(1)} %get-tuple-element.60), channel_id=1, source_target_pairs={{1,0},{2,1},{3,2},{4,3},{5,4},{6,5},{7,6},{9,8},{10,9},{11,10},{12... | collective-permute-start | bytes 7688 | tf_op jit(solution)/shard_map/ppermute | solution.py:22
  73.8 9.8 %collective-permute-start.15 = (f32[10,1,64]{2,1,0:T(1,128)S(1)}, f32[10,1,64]{2,1,0:T(1,128)S(1)}, u32[]{:S(2)}, u32[]{:S(2)}) collective-permute-start(f32[10,1,64]{2,1,0:T(1,128)S(1)} %get-tuple-element.59), channel_id=1, source_target_pairs={{0,1},{1,2},{2,3},{3,4},{4,5},{5,6},{6,7},{8,9},{9,10},{10,11},{11... | collective-permute-start | bytes 7688 | tf_op jit(solution)/shard_map/ppermute | solution.py:21
  78.5 6.5 %collective-permute-start.6 = (f32[18,1,128]{2,1,0:T(1,128)S(1)}, f32[18,1,128]{2,1,0:T(1,128)S(1)}, u32[]{:S(2)}, u32[]{:S(2)}) collective-permute-start(f32[18,1,128]{2,1,0:T(1,128)S(1)} %get-tuple-element.37), channel_id=1, source_target_pairs={{0,1},{1,2},{2,3},{3,4},{4,5},{5,6},{6,7},{8,9},{9,10},{10,11},{11... | collective-permute-start | bytes 27656 | tf_op jit(solution)/shard_map/ppermute | solution.py:21
  98.5 6.2 %collective-permute-start.10 = (f32[18,1,128]{2,1,0:T(1,128)S(1)}, f32[18,1,128]{2,1,0:T(1,128)S(1)}, u32[]{:S(2)}, u32[]{:S(2)}) collective-permute-start(f32[18,1,128]{2,1,0:T(1,128)S(1)} %get-tuple-element.35), channel_id=1, source_target_pairs={{0,1},{1,2},{2,3},{3,4},{4,5},{5,6},{6,7},{8,9},{9,10},{10,11},{11... | collective-permute-start | bytes 27656 | tf_op jit(solution)/shard_map/ppermute | solution.py:21
  142.6 7.3 %collective-permute-start.27 = (f32[6,1,32]{2,1,0:T(1,128)S(1)}, f32[6,1,32]{2,1,0:T(1,128)S(1)}, u32[]{:S(2)}, u32[]{:S(2)}) collective-permute-start(f32[6,1,32]{2,1,0:T(1,128)S(1)} %get-tuple-element.79), channel_id=1, source_target_pairs={{0,1},{1,2},{2,3},{3,4},{4,5},{5,6},{6,7},{8,9},{9,10},{10,11},{11... | collective-permute-start | bytes 2312 | tf_op jit(solution)/shard_map/ppermute | solution.py:21
  163.8 6.0 %collective-permute-start.22 = (f32[10,1,64]{2,1,0:T(1,128)S(1)}, f32[10,1,64]{2,1,0:T(1,128)S(1)}, u32[]{:S(2)}, u32[]{:S(2)}) collective-permute-start(f32[10,1,64]{2,1,0:T(1,128)S(1)} %get-tuple-element.55), channel_id=1, source_target_pairs={{0,1},{1,2},{2,3},{3,4},{4,5},{5,6},{6,7},{8,9},{9,10},{10,11},{11... | collective-permute-start | bytes 7688 | tf_op jit(solution)/shard_map/ppermute | solution.py:21
  185.8 5.9 %collective-permute-start.30 = (f32[6,1,32]{2,1,0:T(1,128)S(1)}, f32[6,1,32]{2,1,0:T(1,128)S(1)}, u32[]{:S(2)}, u32[]{:S(2)}) collective-permute-start(f32[6,1,32]{2,1,0:T(1,128)S(1)} %get-tuple-element.77), channel_id=1, source_target_pairs={{0,1},{1,2},{2,3},{3,4},{4,5},{5,6},{6,7},{8,9},{9,10},{10,11},{11... | collective-permute-start | bytes 2312 | tf_op jit(solution)/shard_map/ppermute | solution.py:21
  203.1 5.9 %collective-permute-start.34 = (f32[6,1,32]{2,1,0:T(1,128)S(1)}, f32[6,1,32]{2,1,0:T(1,128)S(1)}, u32[]{:S(2)}, u32[]{:S(2)}) collective-permute-start(f32[6,1,32]{2,1,0:T(1,128)S(1)} %get-tuple-element.75), channel_id=1, source_target_pairs={{0,1},{1,2},{2,3},{3,4},{4,5},{5,6},{6,7},{8,9},{9,10},{10,11},{11... | collective-permute-start | bytes 2312 | tf_op jit(solution)/shard_map/ppermute | solution.py:21
  213.9 8.6 %collective-permute-start.40 = (f32[1,4,16]{2,1,0:T(4,128)S(1)}, f32[1,4,16]{2,1,0:T(4,128)S(1)}, u32[]{:S(2)}, u32[]{:S(2)}) collective-permute-start(f32[1,4,16]{2,1,0:T(4,128)S(1)} %get-tuple-element.112), channel_id=1, source_target_pairs={{0,8},{8,16},{16,24},{1,9},{9,17},{17,25},{2,10},{10,18},{18,26},{... | collective-permute-start | bytes 776 | tf_op jit(solution)/shard_map/ppermute | solution.py:21
  218.8 8.8 %collective-permute-start.51 = (f32[2,2,8]{2,1,0:T(2,128)S(1)}, f32[2,2,8]{2,1,0:T(2,128)S(1)}, u32[]{:S(2)}, u32[]{:S(2)}) collective-permute-start(f32[2,2,8]{2,1,0:T(2,128)S(1)} %maximum_select_fusion.3), channel_id=1, source_target_pairs={{0,16},{16,0},{8,24},{24,8},{1,17},{17,1},{9,25},{25,9},{2,18},{18... | collective-permute-start | bytes 392 | tf_op jit(solution)/shard_map/ppermute | solution.py:34
  231.9 33.1 %collective-permute-start.44 = (f32[1,4,16]{2,1,0:T(4,128)S(1)}, f32[1,4,16]{2,1,0:T(4,128)S(1)}, u32[]{:S(2)}, u32[]{:S(2)}) collective-permute-start(f32[1,4,16]{2,1,0:T(4,128)S(1)} %get-tuple-element.110), channel_id=1, source_target_pairs={{0,8},{8,16},{16,24},{1,9},{9,17},{17,25},{2,10},{10,18},{18,26},{... | collective-permute-start | bytes 776 | tf_op jit(solution)/shard_map/ppermute | solution.py:21
  233.2 31.8 %collective-permute-start.45 = (f32[1,4,16]{2,1,0:T(4,128)S(1)}, f32[1,4,16]{2,1,0:T(4,128)S(1)}, u32[]{:S(2)}, u32[]{:S(2)}) collective-permute-start(f32[1,4,16]{2,1,0:T(4,128)S(1)} %get-tuple-element.111), channel_id=1, source_target_pairs={{8,0},{16,8},{24,16},{9,1},{17,9},{25,17},{10,2},{18,10},{26,18},{... | collective-permute-start | bytes 776 | tf_op jit(solution)/shard_map/ppermute | solution.py:22
  410.2 5.9 %collective-permute-start.70 = (f32[10,1,64]{2,1,0:T(1,128)S(1)}, f32[10,1,64]{2,1,0:T(1,128)S(1)}, u32[]{:S(2)}, u32[]{:S(2)}) collective-permute-start(f32[10,1,64]{2,1,0:T(1,128)S(1)} %get-tuple-element.53), channel_id=1, source_target_pairs={{0,1},{1,2},{2,3},{3,4},{4,5},{5,6},{6,7},{8,9},{9,10},{10,11},{11... | collective-permute-start | bytes 7688 | tf_op jit(solution)/shard_map/ppermute | solution.py:21
  427.6 6.1 %collective-permute-start.74 = (f32[10,1,64]{2,1,0:T(1,128)S(1)}, f32[10,1,64]{2,1,0:T(1,128)S(1)}, u32[]{:S(2)}, u32[]{:S(2)}) collective-permute-start(f32[10,1,64]{2,1,0:T(1,128)S(1)} %get-tuple-element.51), channel_id=1, source_target_pairs={{0,1},{1,2},{2,3},{3,4},{4,5},{5,6},{6,7},{8,9},{9,10},{10,11},{11... | collective-permute-start | bytes 7688 | tf_op jit(solution)/shard_map/ppermute | solution.py:21
  (65 other events, 670.8 us)
where the time goes:
time: 479 us; the launch traced here: 475 us
  starting transfers between devices  192 us (40%)
  waiting for transfers between devices  106 us (22%)
  blocking collectives  60.8 us (13%)
  other arithmetic  50.2 us (10%)
  local copies, waits for them, and re-layouts  45.2 us (9%)
  between operations  20.9 us (4%)
    ppermute x40, starting transfers between devices, with_halo(): before = lax.ppermute(last, axis, up)  132 us
    ppermute x40, waiting for transfers between devices, with_halo(): after = lax.ppermute(leading, axis, down)  102 us
    all_gather x2, blocking collectives, merge_boxes(): return lax.all_gather(pieces, 'box', axis=1, tiled=True)  60.8 us
    ppermute x40, starting transfers between devices, with_halo(): after = lax.ppermute(leading, axis, down)  52 us
    reshape x4, local copies, waits for them, and re-layouts, restrict_mean(): blocks = field.reshape(size_a // 2, 2, size_b // 2, 2, size_c // 2, 2)  40 us
    reduce_sum x10, other arithmetic, restrict_mean(): return jnp.mean(blocks, axis=(1, 3, 5))  15.5 us
  transfers between devices with their start and end apart: 84, of which 35 were waited for; matrix products, arithmetic and copies ran while one was open for 15% of the time, Pallas kernels for 0%

commit v1 on v0

--- a/solution.py
+++ b/solution.py
@@ -1,11 +1,493 @@
+import functools
+
 import jax
 import jax.numpy as jnp
 from jax import lax
+from jax.experimental import pallas as pl
+from jax.experimental.pallas import tpu as pltpu
 from jax.sharding import PartitionSpec as P
 
 LEVELS = 4
 SWEEPS = 2
 COARSE = 8
+W = 2.0 / 3.0
+MESH = pl.DeviceIdType.MESH
+F32 = jnp.float32
+
+X0, Y0, LANES = 16, 32, 128
+H0 = 4
+H1 = 5
+HY = 8
+DIRS = [(dx, dy) for dx in (-1, 0, 1) for dy in (-1, 0, 1) if (dx, dy) != (0, 0)]
+
+
+def roll(v, shift, axis):
+    return pltpu.roll(v, shift % v.shape[axis], axis)
+
+
+def lane_of(shape):
+    return lax.broadcasted_iota(jnp.int32, shape, len(shape) - 1)
+
+
+def pair_lanes(v, apart):
+    lane = lane_of(v.shape)
+    return v + jnp.where((lane & apart) == 0, roll(v, -apart, 1), roll(v, apart, 1))
+
+
+def span(size, halo, step, own):
+    if step == 0:
+        return (halo, size), (halo, size)
+    if step < 0:
+        return (halo, own), (halo + size, own)
+    return (halo + size - own, own), (0, own)
+
+
+def kernel(
+    G, B, rs_ref, be_ref, out_ref,
+    B0, S0, V0, U0, CX0, CY0, CM0, CP0, Q0, D0,
+    B1, S1, V1, U1, CX1, CY1, CM1, CP1, Q1, D1,
+    T, PB, PS, GB, GS, V2, C2, C3, C4, E, F3,
+    halo_send, halo_recv, ga_send, ga_recv, own_sem, loc_sem,
+):
+    n = G * B
+    g = lax.axis_index("grp")
+    b = lax.axis_index("box")
+    me = g * B + b
+    ry2, ry3, ry4 = 8 * B, 4 * B, 2 * B
+
+    own0 = (pl.ds(H0, X0), pl.ds(HY, Y0))
+    load_b = pltpu.make_async_copy(be_ref, B0.at[own0[0], own0[1]], loc_sem.at[0])
+    load_s = pltpu.make_async_copy(rs_ref, S0.at[own0[0], own0[1]], loc_sem.at[1])
+    load_b.start()
+    load_s.start()
+
+    barrier = pltpu.get_barrier_semaphore()
+
+    def greet(d, carry):
+        peer = (me + d) % n
+        pl.semaphore_signal(barrier, inc=1, device_id=(peer // B, peer % B), device_id_type=MESH)
+        return carry
+
+    lax.fori_loop(1, n, greet, 0)
+
+    for ref, nx, hx, ny in ((B0, X0, H0, Y0), (S0, X0, H0, Y0), (B1, X0 // 2, H1, Y0 // 2), (S1, X0 // 2, H1, Y0 // 2)):
+        rows = ny + 2 * HY
+        planes = nx + 2 * hx
+
+        @pl.when(g == 0)
+        def _():
+            ref[pl.ds(0, hx)] = jnp.zeros((hx, rows, LANES), F32)
+
+        @pl.when(g == G - 1)
+        def _():
+            ref[pl.ds(hx + nx, hx)] = jnp.zeros((hx, rows, LANES), F32)
+
+        @pl.when(b == 0)
+        def _():
+            ref[:, pl.ds(0, HY)] = jnp.zeros((planes, HY, LANES), F32)
+
+        @pl.when(b == B - 1)
+        def _():
+            ref[:, pl.ds(HY + ny, HY)] = jnp.zeros((planes, HY, LANES), F32)
+
+    V2[0] = jnp.zeros((ry2 + 16, LANES), F32)
+    V2[G + 1] = jnp.zeros((ry2 + 16, LANES), F32)
+    V2[:, pl.ds(0, 8)] = jnp.zeros((G + 2, 8, LANES), F32)
+    V2[:, pl.ds(8 + ry2, 8)] = jnp.zeros((G + 2, 8, LANES), F32)
+
+    pl.semaphore_wait(barrier, n - 1)
+
+    def halo_copies(kind, src, dst, nx, hx, ny, src_is_input):
+        made = []
+        for at, (dx, dy) in enumerate(DIRS):
+            (sx, lx), (tx, _) = span(nx, hx, dx, hx)
+            (sy, ly), (ty, _) = span(ny, HY, dy, HY)
+            if src_is_input:
+                sx, sy = sx - hx, sy - HY
+            copy = pltpu.make_async_remote_copy(
+                src_ref=src.at[pl.ds(sx, lx), pl.ds(sy, ly)],
+                dst_ref=dst.at[pl.ds(tx, lx), pl.ds(ty, ly)],
+                send_sem=halo_send.at[kind, at],
+                recv_sem=halo_recv.at[kind, at],
+                device_id=(g + dx, b + dy),
+                device_id_type=MESH,
+            )
+            there = (g + dx >= 0) & (g + dx < G) & (b + dy >= 0) & (b + dy < B)
+            here = (g - dx >= 0) & (g - dx < G) & (b - dy >= 0) & (b - dy < B)
+            made.append((copy, there, here))
+        return made
+
+    def start_all(copies):
+        for copy, there, _ in copies:
+            pl.when(there)(copy.start)
+
+    def recv_all(copies):
+        for copy, _, here in copies:
+            pl.when(here)(copy.wait_recv)
+
+    def sent_all(copies):
+        for copy, there, _ in copies:
+            pl.when(there)(copy.wait_send)
+
+    def gather_start(which, packed, whole):
+        pltpu.make_async_copy(packed, whole.at[g, pl.ds(pl.multiple_of(b * 8, 8), 8)], ga_recv.at[which]).start()
+
+        def one(d, carry):
+            peer = (me + d) % n
+            pltpu.make_async_remote_copy(
+                src_ref=packed,
+                dst_ref=whole.at[g, pl.ds(pl.multiple_of(b * 8, 8), 8)],
+                send_sem=ga_send.at[which, d],
+                recv_sem=ga_recv.at[which],
+                device_id=(peer // B, peer % B),
+                device_id_type=MESH,
+            ).start()
+            return carry
+
+        lax.fori_loop(1, n, one, 0)
+
+    def gather_recv(which, whole):
+        pltpu.make_async_copy(whole, whole, ga_recv.at[which]).wait()
+
+    def gather_sent(which, packed):
+        def one(d, carry):
+            pltpu.make_async_copy(packed, packed, ga_send.at[which, d]).wait()
+            return carry
+
+        lax.fori_loop(1, n, one, 0)
+
+    beta_halo = halo_copies(0, be_ref, B0, X0, H0, Y0, True)
+    source_halo = halo_copies(1, rs_ref, S0, X0, H0, Y0, True)
+    start_all(beta_halo)
+    start_all(source_halo)
+    load_b.wait()
+
+    def halve(pair, apart, slot):
+        rows = pair.shape[0]
+        T[slot, pl.ds(0, rows)] = pair_lanes(pair, apart)
+        return 0.125 * (T[slot, pl.ds(0, rows // 2, stride=2)] + T[slot, pl.ds(1, rows // 2, stride=2)])
+
+    def pack(planes):
+        lane = lane_of(planes[0].shape) & 3
+        packed = planes[3]
+        for k in (2, 1, 0):
+            packed = jnp.where(lane == k, planes[k], packed)
+        return packed
+
+    for p in range(X0 // 2):
+        B1[H1 + p, pl.ds(HY, Y0 // 2)] = halve(
+            B0[H0 + 2 * p, pl.ds(HY, Y0)] + B0[H0 + 2 * p + 1, pl.ds(HY, Y0)], 1, p
+        )
+    beta1_halo = halo_copies(2, B1, B1, X0 // 2, H1, Y0 // 2, False)
+    start_all(beta1_halo)
+    PB[...] = pack([
+        halve(B1[H1 + 2 * p, pl.ds(HY, Y0 // 2)] + B1[H1 + 2 * p + 1, pl.ds(HY, Y0 // 2)], 2, p)
+        for p in range(X0 // 4)
+    ])
+    gather_start(0, PB, GB)
+
+    def setup(level, Bl, CX, CY, CM, CP, Q, D, first, last, row, rows, hx, nx, ny):
+        apart = 1 << level
+        h = 0.5 * 0.25**level
+
+        def plane(i, carry):
+            at = pl.ds(row, rows)
+            c = Bl[i, at]
+            xm = Bl[i - 1, at]
+            xp = Bl[i + 1, at]
+            ym = Bl[i, pl.ds(row - 1, rows)]
+            yp = Bl[i, pl.ds(row + 1, rows)]
+            lane = lane_of(c.shape)
+            low = lane >= apart
+            high = lane < LANES - apart
+            zm = jnp.where(low, roll(c, apart, 1), 0.0)
+            zp = jnp.where(high, roll(c, -apart, 1), 0.0)
+            CX[i, at] = h * (c + xm)
+            CY[i, at] = h * (c + ym)
+            CM[i, at] = jnp.where(low, h * (c + zm), 0.0)
+            CP[i, at] = jnp.where(high, h * (c + zp), 0.0)
+            d = h * (6.0 * c + ((xm + xp) + (ym + yp) + (zm + zp)))
+            D[i, at] = d
+            x = g * nx + i - hx
+            y = lax.broadcasted_iota(jnp.int32, c.shape, 0) + (b * ny + row - HY)
+            inside = (y >= 0) & (y < B * ny) & (x >= 0) & (x < G * nx)
+            Q[i, at] = jnp.where(inside, W / d, 0.0)
+            return carry
+
+        lax.fori_loop(first, last, plane, 0)
+
+    def across(level, V, CX, CY, CM, CP, i, row, rows):
+        apart = 1 << level
+        at = pl.ds(row, rows)
+        up = pl.ds(row + 1, rows)
+        v = V[i, at]
+        total = CX[i, at] * V[i - 1, at] + CX[i + 1, at] * V[i + 1, at]
+        total = total + (CY[i, at] * V[i, pl.ds(row - 1, rows)] + CY[i, up] * V[i, up])
+        total = total + (CM[i, at] * roll(v, apart, 1) + CP[i, at] * roll(v, -apart, 1))
+        return v, total
+
+    def first_sweep(V, Q, S, first, last, row, rows):
+        def plane(i, carry):
+            V[i, pl.ds(row, rows)] = Q[i, pl.ds(row, rows)] * S[i, pl.ds(row, rows)]
+            return carry
+
+        lax.fori_loop(first, last, plane, 0)
+
+    def sweep(level, V, U, S, Q, coeffs, first, last, row, rows, drop_x=0, drop_y=0):
+        def plane(i, carry):
+            v, total = across(level, V, *coeffs, i, row, rows)
+            U[i - drop_x, pl.ds(row - drop_y, rows)] = (1.0 - W) * v + Q[i, pl.ds(row, rows)] * (
+                S[i, pl.ds(row, rows)] + total
+            )
+            return carry
+
+        lax.fori_loop(first, last, plane, 0)
+
+    def residual(level, V, S, D, coeffs, i, row, rows):
+        v, total = across(level, V, *coeffs, i, row, rows)
+        return S[i, pl.ds(row, rows)] - (D[i, pl.ds(row, rows)] * v - total)
+
+    coeffs0 = (CX0, CY0, CM0, CP0)
+    coeffs1 = (CX1, CY1, CM1, CP1)
+    row0, rows0 = 4, 40
+    row1, rows1 = 4, 24
+
+    recv_all(beta_halo)
+    setup(0, B0, CX0, CY0, CM0, CP0, Q0, D0, 1, 23, row0, rows0, H0, X0, Y0)
+    load_s.wait()
+    recv_all(source_halo)
+    first_sweep(V0, Q0, S0, 1, 23, row0, rows0)
+    sweep(0, V0, U0, S0, Q0, coeffs0, 2, 22, row0, rows0)
+
+    def down0(p, carry):
+        i = H0 + 2 * p
+        pair = residual(0, U0, S0, D0, coeffs0, i, HY, Y0) + residual(0, U0, S0, D0, coeffs0, i + 1, HY, Y0)
+        S1[H1 + p, pl.ds(HY, Y0 // 2)] = halve(pair, 1, p)
+        return carry
+
+    lax.fori_loop(0, X0 // 2, down0, 0)
+    source1_halo = halo_copies(3, S1, S1, X0 // 2, H1, Y0 // 2, False)
+    start_all(source1_halo)
+
+    recv_all(beta1_halo)
+    setup(1, B1, CX1, CY1, CM1, CP1, Q1, D1, 1, 17, row1, rows1, H1, X0 // 2, Y0 // 2)
+    recv_all(source1_halo)
+    first_sweep(V1, Q1, S1, 1, 17, row1, rows1)
+    sweep(1, V1, U1, S1, Q1, coeffs1, 2, 16, row1, rows1)
+    planes = []
+    for p in range(X0 // 4):
+        i = H1 + 2 * p
+        pair = residual(1, U1, S1, D1, coeffs1, i, HY, Y0 // 2) + residual(1, U1, S1, D1, coeffs1, i + 1, HY, Y0 // 2)
+        planes.append(halve(pair, 2, p))
+    PS[...] = pack(planes)
+    gather_start(1, PS, GS)
+
+    def neighbours(v, level):
+        st, zs = 1 << (level - 2), 1 << level
+        before = [v[i - 1] for i in range(G)]
+        after = [v[(i + 1) % G] for i in range(G)]
+        if st == 4:
+            xm, xp = before, after
+        else:
+            k = lane_of(v[0].shape) & 3
+            xm = [jnp.where(k >= st, roll(v[i], st, 1), roll(before[i], st - 4, 1)) for i in range(G)]
+            xp = [jnp.where(k < 4 - st, roll(v[i], -st, 1), roll(after[i], 4 - st, 1)) for i in range(G)]
+        ym = [roll(a, 1, 0) for a in v]
+        yp = [roll(a, -1, 0) for a in v]
+        zm = [roll(a, zs, 1) for a in v]
+        zp = [roll(a, -zs, 1) for a in v]
+        return xm, xp, ym, yp, zm, zp
+
+    def setup_whole(beta, C, level):
+        st, zs = 1 << (level - 2), 1 << level
+        h = 0.5 * 0.25**level
+        near = neighbours(beta, level)
+        shape = beta[0].shape
+        lane = lane_of(shape)
+        row = lax.broadcasted_iota(jnp.int32, shape, 0)
+        for i in range(G):
+            ok = [
+                ((lane & 3) >= st) if i == 0 else None,
+                ((lane & 3) < 4 - st) if i == G - 1 else None,
+                row > 0,
+                row < shape[0] - 1,
+                lane >= zs,
+                lane < LANES - zs,
+            ]
+            total = 6.0 * beta[i]
+            for d in range(6):
+                there = near[d][i] if ok[d] is None else jnp.where(ok[d], near[d][i], 0.0)
+                total = total + there
+                face = h * (beta[i] + there)
+                C[d, i] = face if ok[d] is None else jnp.where(ok[d], face, 0.0)
+            diag = h * total
+            C[6, i] = diag
+            C[7, i] = W / diag
+
+    def sum_across(v, C, level):
+        near = neighbours(v, level)
+        out = []
+        for i in range(G):
+            out.append(
+                (C[0, i] * near[0][i] + C[1, i] * near[1][i])
+                + (C[2, i] * near[2][i] + C[3, i] * near[3][i])
+                + (C[4, i] * near[4][i] + C[5, i] * near[5][i])
+            )
+        return out
+
+    def sweep_whole(v, s, C, level):
+        total = sum_across(v, C, level)
+        return [(1.0 - W) * v[i] + C[7, i] * (s[i] + total[i]) for i in range(G)]
+
+    def coarsen(v, level):
+        st, zs = 1 << (level - 2), 1 << level
+        rows = v[0].shape[0]
+        out = []
+        for i in range(G):
+            E[i, pl.ds(0, rows)] = pair_lanes(pair_lanes(v[i], st), zs)
+            out.append(0.125 * (E[i, pl.ds(0, rows // 2, stride=2)] + E[i, pl.ds(1, rows // 2, stride=2)]))
+        return out
+
+    def refine(v):
+        rows = v[0].shape[0]
+        out = []
+        for i in range(G):
+            E[i, pl.ds(0, rows, stride=2)] = v[i]
+            E[i, pl.ds(1, rows, stride=2)] = v[i]
+            out.append(E[i, pl.ds(0, 2 * rows)])
+        return out
+
+    gather_recv(0, GB)
+    beta2 = [GB[i] for i in range(G)]
+    setup_whole(beta2, C2, 2)
+    beta3 = coarsen(beta2, 2)
+    setup_whole(beta3, C3, 3)
+    beta4 = coarsen(beta3, 3)
+    setup_whole(beta4, C4, 4)
+
+    gather_recv(1, GS)
+    s2 = [GS[i] for i in range(G)]
+    v = [C2[7, i] * s2[i] for i in range(G)]
+    v = sweep_whole(v, s2, C2, 2)
+    for i in range(G):
+        V2[i + 1, pl.ds(8, ry2)] = v[i]
+    total = sum_across(v, C2, 2)
+    s3 = coarsen([s2[i] - (C2[6, i] * v[i] - total[i]) for i in range(G)], 2)
+    v = [C3[7, i] * s3[i] for i in range(G)]
+    v = sweep_whole(v, s3, C3, 3)
+    for i in range(G):
+        F3[0, i] = v[i]
+        F3[1, i] = s3[i]
+    total = sum_across(v, C3, 3)
+    s4 = coarsen([s3[i] - (C3[6, i] * v[i] - total[i]) for i in range(G)], 3)
+
+    def dot(a, c):
+        acc = a[0] * c[0]
+        for i in range(1, G):
+            acc = acc + a[i] * c[i]
+        part = acc[0:8]
+        for j in range(8, ry4, 8):
+            part = part + acc[j : j + 8]
+        return jnp.sum(jnp.sum(part, axis=0, keepdims=True), axis=1, keepdims=True)
+
+    def cg(step, carry):
+        x, r, p, rr = carry
+        near = sum_across(p, C4, 4)
+        q = [C4[6, i] * p[i] - near[i] for i in range(G)]
+        alpha = rr / dot(p, q)
+        x = [x[i] + alpha * p[i] for i in range(G)]
+        r = [r[i] - alpha * q[i] for i in range(G)]
+        new = dot(r, r)
+        ratio = new / rr
+        p = [r[i] + ratio * p[i] for i in range(G)]
+        return x, r, p, new
+
+    zero = [jnp.zeros((ry4, LANES), F32) for i in range(G)]
+    x4 = lax.fori_loop(0, COARSE, cg, (zero, s4, s4, dot(s4, s4)))[0]
+
+    up = refine(x4)
+    s3 = [F3[1, i] for i in range(G)]
+    v = [F3[0, i] + up[i] for i in range(G)]
+    for _ in range(SWEEPS):
+        v = sweep_whole(v, s3, C3, 3)
+    up = refine(v)
+    s2 = [GS[i] for i in range(G)]
+    v = [V2[i + 1, pl.ds(8, ry2)] + up[i] for i in range(G)]
+    for _ in range(SWEEPS):
+        v = sweep_whole(v, s2, C2, 2)
+    for i in range(G):
+        V2[i + 1, pl.ds(8, ry2)] = v[i]
+
+    for x2 in range(-2, 6):
+        k = x2 % 4
+        window = V2[g + 1 + x2 // 4, pl.ds(pl.multiple_of(b * 8, 8), 24)]
+        one = jnp.where((lane_of(window.shape) & 3) == k, window, 0.0)
+        one = one + roll(one, 1 if k in (0, 2) else -1, 1)
+        one = one + roll(one, 2 if k in (0, 1) else -2, 1)
+        T[x2 + 2, pl.ds(0, 24)] = one
+    for x2 in range(-2, 6):
+        add = T[x2 + 2, pl.ds(6, 12)]
+        for i in (2 * x2 + 5, 2 * x2 + 6):
+            if 2 <= i < 16:
+                for odd in (0, 1):
+                    at = pl.ds(row1 + odd, 12, stride=2)
+                    U1[i, at] = U1[i, at] + add
+    sweep(1, U1, V1, S1, Q1, coeffs1, 3, 15, row1, rows1)
+    sweep(1, V1, U1, S1, Q1, coeffs1, 4, 14, row1, rows1)
+
+    def prolong0(i, carry):
+        add = U1[i + 3, pl.ds(6, 20)]
+        for half in (0, 1):
+            for odd in (0, 1):
+                at = pl.ds(row0 + odd, 20, stride=2)
+                U0[2 * i + half, at] = U0[2 * i + half, at] + add
+        return carry
+
+    lax.fori_loop(1, 11, prolong0, 0)
+    sweep(0, U0, V0, S0, Q0, coeffs0, 3, 21, row0, rows0)
+    sweep(0, V0, out_ref, S0, Q0, coeffs0, 4, 20, HY, Y0, H0, HY)
+
+    sent_all(beta_halo)
+    sent_all(source_halo)
+    sent_all(beta1_halo)
+    sent_all(source1_halo)
+    gather_sent(0, PB)
+    gather_sent(1, PS)
+
+
+def in_one_kernel(G, B, right_side, beta):
+    level0 = pltpu.VMEM((X0 + 2 * H0, Y0 + 2 * HY, LANES), F32)
+    level1 = pltpu.VMEM((X0 // 2 + 2 * H1, Y0 // 2 + 2 * HY, LANES), F32)
+    return pl.pallas_call(
+        functools.partial(kernel, G, B),
+        out_shape=jax.ShapeDtypeStruct(right_side.shape, F32),
+        in_specs=[pl.BlockSpec(memory_space=pl.ANY)] * 2,
+        out_specs=pl.BlockSpec(memory_space=pltpu.VMEM),
+        scratch_shapes=[level0] * 10
+        + [level1] * 10
+        + [
+            pltpu.VMEM((8, Y0, LANES), F32),
+            pltpu.VMEM((8, LANES), F32),
+            pltpu.VMEM((8, LANES), F32),
+            pltpu.VMEM((G, 8 * B, LANES), F32),
+            pltpu.VMEM((G, 8 * B, LANES), F32),
+            pltpu.VMEM((G + 2, 8 * B + 16, LANES), F32),
+            pltpu.VMEM((8, G, 8 * B, LANES), F32),
+            pltpu.VMEM((8, G, 4 * B, LANES), F32),
+            pltpu.VMEM((8, G, 2 * B, LANES), F32),
+            pltpu.VMEM((G, 8 * B, LANES), F32),
+            pltpu.VMEM((2, G, 4 * B, LANES), F32),
+            pltpu.SemaphoreType.DMA((4, 8)),
+            pltpu.SemaphoreType.DMA((4, 8)),
+            pltpu.SemaphoreType.DMA((2, G * B)),
+            pltpu.SemaphoreType.DMA((2,)),
+            pltpu.SemaphoreType.DMA((1,)),
+            pltpu.SemaphoreType.DMA((2,)),
+        ],
+        compiler_params=pltpu.CompilerParams(
+            collective_id=0, has_side_effects=True, vmem_limit_bytes=40 * 1024 * 1024
+        ),
+    )(right_side, beta)
 
 
 relax_weight = 2.0 / 3.0
@@ -170,7 +652,13 @@
 
 
 def solution(mesh):
-    placed = (P("grp", "box", None), P("grp", "box", None))
-    return jax.shard_map(
-        shards, mesh=mesh, in_specs=placed, out_specs=P("grp", "box", None), check_vma=False
-    )
+    placed = P("grp", "box", None)
+    G, B = mesh.shape["grp"], mesh.shape["box"]
+    small = G * B <= 64 and (2 * B) % 8 == 0 and G > 1
+
+    def local(right_side, beta):
+        if small and right_side.shape == (X0, Y0, LANES):
+            return in_one_kernel(G, B, right_side, beta)
+        return shards(right_side, beta)
+
+    return jax.shard_map(local, mesh=mesh, in_specs=(placed, placed), out_specs=placed, check_vma=False)

time: 479 us -> 47.1 us (0.10)
  starting transfers between devices: 192 us -> 0 us
  waiting for transfers between devices: 106 us -> 0 us
  blocking collectives: 60.8 us -> 0 us
  other arithmetic: 50.2 us -> 0 us
  Pallas kernels: 0 us -> 44.3 us
  local copies, waits for them, and re-layouts: 45.2 us -> 2.6 us
  between operations: 20.9 us -> 0.01 us
    ppermute x84 -> x0, starting transfers between devices: 192 us -> none  [the longest x40 132 us: with_halo(): before = lax.ppermute(last, axis, up)]
    ppermute x84 -> x0, waiting for transfers between devices: 106 us -> none  [the longest x40 102 us: with_halo(): after = lax.ppermute(leading, axis, down)]
    all_gather x2 -> x0, blocking collectives: 60.8 us -> none  [merge_boxes(): return lax.all_gather(pieces, 'box', axis=1, tiled=True)]
    pallas_call x0 -> x1, Pallas kernels: none -> 44.3 us  [in_one_kernel(): pl.pallas_call(functools.partial(kernel, G, B), out_shape=jax.ShapeDtypeS...]
    reshape x10 -> x0, local copies, waits for them, and re-layouts: 41.1 us -> none  [the longest x4 40 us: restrict_mean(): blocks = field.reshape(size_a // 2, 2, size_b // 2, 2, size_c // 2, 2)]
    reduce_sum x26 -> x0, other arithmetic: 26.6 us -> none  [the longest x10 15.5 us: restrict_mean(): return jnp.mean(blocks, axis=(1, 3, 5))]
    add x23 -> x0, other arithmetic: 9.19 us -> none  [the longest x12 7.17 us: jacobi_sweeps(): field + relax_weight * (source - apply_operator(padder(field), coeffs, sc...]
    mul x20 -> x0, other arithmetic: 5.5 us -> none  [the longest x4 2.2 us: shards(): field = relax_weight * source * inverse]
  transfers between devices with their start and end apart: 84 -> 0, of which waited for: 35 -> 0; matrix products, arithmetic and copies ran while one was open for 15% -> 0% of each run, Pallas kernels for 0% -> 0%
where the time goes in v1:
time: 47.1 us; the launch traced here: 46.9 us
  Pallas kernels  44.3 us (94%)
  local copies, waits for them, and re-layouts  2.6 us (6%)
    pallas_call x1, Pallas kernels, in_one_kernel(): pl.pallas_call(functools.partial(kernel, G, B), out_shape=jax.ShapeDtypeS...  44.3 us
    unnamed x5, local copies, waits for them, and re-layouts  2.6 us

profile of v1, /device:TPU:0, one launch (start us, length us, event | category | flops | bytes accessed | tf_op | source)
XLA Modules:
  0.0 46.9 jit_solution(7466363874075509622)
XLA Ops:
  0.0 0.0 copy-start
  0.0 0.9 %copy-done = f32[16,32,128]{2,1,0:T(8,128)S(1)} copy-done((f32[16,32,128]{2,1,0:T(8,128)S(1)}, f32[16,32,128]{2,1,0:T(8,128)}, u32[]{:S(2)}) %copy-start) | copy-done | bytes 262168
  1.0 0.0 copy-start.1
  1.0 0.9 %copy-done.1 = f32[16,32,128]{2,1,0:T(8,128)S(1)} copy-done((f32[16,32,128]{2,1,0:T(8,128)S(1)}, f32[16,32,128]{2,1,0:T(8,128)}, u32[]{:S(2)}) %copy-start.1) | copy-done | bytes 262168
  1.9 44.3 %shard_map.28 = f32[16,32,128]{2,1,0:T(8,128)S(1)} custom-call(f32[16,32,128]{2,1,0:T(8,128)S(1)} %copy-done, f32[16,32,128]{2,1,0:T(8,128)S(1)} %copy-done.1), custom_call_target="tpu_custom_call" | custom-call | tf_op jit(solution)/shard_map/pallas_call | solution.py:461
  46.2 0.7 %copy.4 = f32[16,32,128]{2,1,0:T(8,128)} copy(f32[16,32,128]{2,1,0:T(8,128)S(1)} %shard_map.28) | data formatting | bytes 524288
Async XLA Ops:
  0.0 0.9 %copy-start = (f32[16,32,128]{2,1,0:T(8,128)S(1)}, f32[16,32,128]{2,1,0:T(8,128)}, u32[]{:S(2)}) copy-start(f32[16,32,128]{2,1,0:T(8,128)} %rs_ref.1) | copy-start | bytes 786436
  1.0 0.9 %copy-start.1 = (f32[16,32,128]{2,1,0:T(8,128)S(1)}, f32[16,32,128]{2,1,0:T(8,128)}, u32[]{:S(2)}) copy-start(f32[16,32,128]{2,1,0:T(8,128)} %be_ref.1) | copy-start | bytes 786436

commit v2 on v1

--- a/solution.py
+++ b/solution.py
@@ -39,7 +39,7 @@
         return (halo, size), (halo, size)
     if step < 0:
         return (halo, own), (halo + size, own)
-    return (halo + size - own, own), (0, own)
+    return (halo + size - own, own), (halo - own, own)
 
 
 def kernel(
@@ -97,11 +97,11 @@
 
     pl.semaphore_wait(barrier, n - 1)
 
-    def halo_copies(kind, src, dst, nx, hx, ny, src_is_input):
+    def halo_copies(kind, src, dst, nx, hx, ny, deep, tall, src_is_input):
         made = []
         for at, (dx, dy) in enumerate(DIRS):
-            (sx, lx), (tx, _) = span(nx, hx, dx, hx)
-            (sy, ly), (ty, _) = span(ny, HY, dy, HY)
+            (sx, lx), (tx, _) = span(nx, hx, dx, deep)
+            (sy, ly), (ty, _) = span(ny, HY, dy, tall)
             if src_is_input:
                 sx, sy = sx - hx, sy - HY
             copy = pltpu.make_async_remote_copy(
@@ -156,8 +156,8 @@
 
         lax.fori_loop(1, n, one, 0)
 
-    beta_halo = halo_copies(0, be_ref, B0, X0, H0, Y0, True)
-    source_halo = halo_copies(1, rs_ref, S0, X0, H0, Y0, True)
+    beta_halo = halo_copies(0, be_ref, B0, X0, H0, Y0, 4, 4, True)
+    source_halo = halo_copies(1, rs_ref, S0, X0, H0, Y0, 3, 4, True)
     start_all(beta_halo)
     start_all(source_halo)
     load_b.wait()
@@ -178,7 +178,7 @@
         B1[H1 + p, pl.ds(HY, Y0 // 2)] = halve(
             B0[H0 + 2 * p, pl.ds(HY, Y0)] + B0[H0 + 2 * p + 1, pl.ds(HY, Y0)], 1, p
         )
-    beta1_halo = halo_copies(2, B1, B1, X0 // 2, H1, Y0 // 2, False)
+    beta1_halo = halo_copies(2, B1, B1, X0 // 2, H1, Y0 // 2, 5, 8, False)
     start_all(beta1_halo)
     PB[...] = pack([
         halve(B1[H1 + 2 * p, pl.ds(HY, Y0 // 2)] + B1[H1 + 2 * p + 1, pl.ds(HY, Y0 // 2)], 2, p)
@@ -214,7 +214,7 @@
             Q[i, at] = jnp.where(inside, W / d, 0.0)
             return carry
 
-        lax.fori_loop(first, last, plane, 0)
+        lax.fori_loop(first, last, plane, 0, unroll=True)
 
     def across(level, V, CX, CY, CM, CP, i, row, rows):
         apart = 1 << level
@@ -231,7 +231,7 @@
             V[i, pl.ds(row, rows)] = Q[i, pl.ds(row, rows)] * S[i, pl.ds(row, rows)]
             return carry
 
-        lax.fori_loop(first, last, plane, 0)
+        lax.fori_loop(first, last, plane, 0, unroll=True)
 
     def sweep(level, V, U, S, Q, coeffs, first, last, row, rows, drop_x=0, drop_y=0):
         def plane(i, carry):
@@ -241,7 +241,7 @@
             )
             return carry
 
-        lax.fori_loop(first, last, plane, 0)
+        lax.fori_loop(first, last, plane, 0, unroll=True)
 
     def residual(level, V, S, D, coeffs, i, row, rows):
         v, total = across(level, V, *coeffs, i, row, rows)
@@ -265,8 +265,8 @@
         S1[H1 + p, pl.ds(HY, Y0 // 2)] = halve(pair, 1, p)
         return carry
 
-    lax.fori_loop(0, X0 // 2, down0, 0)
-    source1_halo = halo_copies(3, S1, S1, X0 // 2, H1, Y0 // 2, False)
+    lax.fori_loop(0, X0 // 2, down0, 0, unroll=True)
+    source1_halo = halo_copies(3, S1, S1, X0 // 2, H1, Y0 // 2, 4, 4, False)
     start_all(source1_halo)
 
     recv_all(beta1_halo)
@@ -443,7 +443,7 @@
                 U0[2 * i + half, at] = U0[2 * i + half, at] + add
         return carry
 
-    lax.fori_loop(1, 11, prolong0, 0)
+    lax.fori_loop(1, 11, prolong0, 0, unroll=True)
     sweep(0, U0, V0, S0, Q0, coeffs0, 3, 21, row0, rows0)
     sweep(0, V0, out_ref, S0, Q0, coeffs0, 4, 20, HY, Y0, H0, HY)
 

time: 47.1 us -> 35.2 us (0.75)
  Pallas kernels: 44.3 us -> 32.4 us
    pallas_call x1, Pallas kernels: 44.3 us -> 32.4 us  [in_one_kernel(): pl.pallas_call(functools.partial(kernel, G, B), out_shape=jax.ShapeDtypeS...]
where the time goes in v2:
time: 35.2 us; the launch traced here: 35 us
  Pallas kernels  32.4 us (92%)
  local copies, waits for them, and re-layouts  2.6 us (7%)
    pallas_call x1, Pallas kernels, in_one_kernel(): pl.pallas_call(functools.partial(kernel, G, B), out_shape=jax.ShapeDtypeS...  32.4 us
    unnamed x5, local copies, waits for them, and re-layouts  2.6 us

profile of v2, /device:TPU:0, one launch (start us, length us, event | category | flops | bytes accessed | tf_op | source)
XLA Modules:
  0.0 35.0 jit_solution(8056104669047010363)
XLA Ops:
  0.0 0.0 copy-start
  0.0 0.9 %copy-done = f32[16,32,128]{2,1,0:T(8,128)S(1)} copy-done((f32[16,32,128]{2,1,0:T(8,128)S(1)}, f32[16,32,128]{2,1,0:T(8,128)}, u32[]{:S(2)}) %copy-start) | copy-done | bytes 262168
  1.0 0.0 copy-start.1
  1.0 0.9 %copy-done.1 = f32[16,32,128]{2,1,0:T(8,128)S(1)} copy-done((f32[16,32,128]{2,1,0:T(8,128)S(1)}, f32[16,32,128]{2,1,0:T(8,128)}, u32[]{:S(2)}) %copy-start.1) | copy-done | bytes 262168
  1.9 32.4 %shard_map.28 = f32[16,32,128]{2,1,0:T(8,128)S(1)} custom-call(f32[16,32,128]{2,1,0:T(8,128)S(1)} %copy-done, f32[16,32,128]{2,1,0:T(8,128)S(1)} %copy-done.1), custom_call_target="tpu_custom_call" | custom-call | tf_op jit(solution)/shard_map/pallas_call | solution.py:461
  34.3 0.7 %copy.4 = f32[16,32,128]{2,1,0:T(8,128)} copy(f32[16,32,128]{2,1,0:T(8,128)S(1)} %shard_map.28) | data formatting | bytes 524288
Async XLA Ops:
  0.0 0.9 %copy-start = (f32[16,32,128]{2,1,0:T(8,128)S(1)}, f32[16,32,128]{2,1,0:T(8,128)}, u32[]{:S(2)}) copy-start(f32[16,32,128]{2,1,0:T(8,128)} %rs_ref.1) | copy-start | bytes 786436
  1.0 0.9 %copy-start.1 = (f32[16,32,128]{2,1,0:T(8,128)S(1)}, f32[16,32,128]{2,1,0:T(8,128)}, u32[]{:S(2)}) copy-start(f32[16,32,128]{2,1,0:T(8,128)} %be_ref.1) | copy-start | bytes 786436

commit v3 on v2

--- a/solution.py
+++ b/solution.py
@@ -97,10 +97,10 @@
 
     pl.semaphore_wait(barrier, n - 1)
 
-    def halo_copies(kind, src, dst, nx, hx, ny, deep, tall, src_is_input):
+    def halo_copies(kind, src, dst, nx, hx, ny, deep, corner, tall, src_is_input):
         made = []
         for at, (dx, dy) in enumerate(DIRS):
-            (sx, lx), (tx, _) = span(nx, hx, dx, deep)
+            (sx, lx), (tx, _) = span(nx, hx, dx, deep if dy == 0 else corner)
             (sy, ly), (ty, _) = span(ny, HY, dy, tall)
             if src_is_input:
                 sx, sy = sx - hx, sy - HY
@@ -156,8 +156,8 @@
 
         lax.fori_loop(1, n, one, 0)
 
-    beta_halo = halo_copies(0, be_ref, B0, X0, H0, Y0, 4, 4, True)
-    source_halo = halo_copies(1, rs_ref, S0, X0, H0, Y0, 3, 4, True)
+    beta_halo = halo_copies(0, be_ref, B0, X0, H0, Y0, 4, 3, 4, True)
+    source_halo = halo_copies(1, rs_ref, S0, X0, H0, Y0, 3, 2, 4, True)
     start_all(beta_halo)
     start_all(source_halo)
     load_b.wait()
@@ -178,13 +178,11 @@
         B1[H1 + p, pl.ds(HY, Y0 // 2)] = halve(
             B0[H0 + 2 * p, pl.ds(HY, Y0)] + B0[H0 + 2 * p + 1, pl.ds(HY, Y0)], 1, p
         )
-    beta1_halo = halo_copies(2, B1, B1, X0 // 2, H1, Y0 // 2, 5, 8, False)
-    start_all(beta1_halo)
+    beta1_halo = halo_copies(2, B1, B1, X0 // 2, H1, Y0 // 2, 5, 5, 8, False)
     PB[...] = pack([
         halve(B1[H1 + 2 * p, pl.ds(HY, Y0 // 2)] + B1[H1 + 2 * p + 1, pl.ds(HY, Y0 // 2)], 2, p)
         for p in range(X0 // 4)
     ])
-    gather_start(0, PB, GB)
 
     def setup(level, Bl, CX, CY, CM, CP, Q, D, first, last, row, rows, hx, nx, ny):
         apart = 1 << level
@@ -256,6 +254,8 @@
     setup(0, B0, CX0, CY0, CM0, CP0, Q0, D0, 1, 23, row0, rows0, H0, X0, Y0)
     load_s.wait()
     recv_all(source_halo)
+    start_all(beta1_halo)
+    gather_start(0, PB, GB)
     first_sweep(V0, Q0, S0, 1, 23, row0, rows0)
     sweep(0, V0, U0, S0, Q0, coeffs0, 2, 22, row0, rows0)
 
@@ -266,7 +266,7 @@
         return carry
 
     lax.fori_loop(0, X0 // 2, down0, 0, unroll=True)
-    source1_halo = halo_copies(3, S1, S1, X0 // 2, H1, Y0 // 2, 4, 4, False)
+    source1_halo = halo_copies(3, S1, S1, X0 // 2, H1, Y0 // 2, 4, 4, 4, False)
     start_all(source1_halo)
 
     recv_all(beta1_halo)

time: 35.2 us -> 34 us (0.966)
  Pallas kernels: 32.4 us -> 31.3 us
    pallas_call x1, Pallas kernels: 32.4 us -> 31.3 us  [in_one_kernel(): pl.pallas_call(functools.partial(kernel, G, B), out_shape=jax.ShapeDtypeS...]
where the time goes in v3:
time: 34 us; the launch traced here: 33.9 us
  Pallas kernels  31.3 us (92%)
  local copies, waits for them, and re-layouts  2.6 us (8%)
    pallas_call x1, Pallas kernels, in_one_kernel(): pl.pallas_call(functools.partial(kernel, G, B), out_shape=jax.ShapeDtypeS...  31.3 us
    unnamed x5, local copies, waits for them, and re-layouts  2.6 us

profile of v3, /device:TPU:0, one launch (start us, length us, event | category | flops | bytes accessed | tf_op | source)
XLA Modules:
  0.0 33.9 jit_solution(12228069013467789377)
XLA Ops:
  0.0 0.0 copy-start
  0.0 0.9 %copy-done = f32[16,32,128]{2,1,0:T(8,128)S(1)} copy-done((f32[16,32,128]{2,1,0:T(8,128)S(1)}, f32[16,32,128]{2,1,0:T(8,128)}, u32[]{:S(2)}) %copy-start) | copy-done | bytes 262168
  1.0 0.0 copy-start.1
  1.0 0.9 %copy-done.1 = f32[16,32,128]{2,1,0:T(8,128)S(1)} copy-done((f32[16,32,128]{2,1,0:T(8,128)S(1)}, f32[16,32,128]{2,1,0:T(8,128)}, u32[]{:S(2)}) %copy-start.1) | copy-done | bytes 262168
  1.9 31.3 %shard_map.28 = f32[16,32,128]{2,1,0:T(8,128)S(1)} custom-call(f32[16,32,128]{2,1,0:T(8,128)S(1)} %copy-done, f32[16,32,128]{2,1,0:T(8,128)S(1)} %copy-done.1), custom_call_target="tpu_custom_call" | custom-call | tf_op jit(solution)/shard_map/pallas_call | solution.py:461
  33.2 0.7 %copy.4 = f32[16,32,128]{2,1,0:T(8,128)} copy(f32[16,32,128]{2,1,0:T(8,128)S(1)} %shard_map.28) | data formatting | bytes 524288
Async XLA Ops:
  0.0 0.9 %copy-start = (f32[16,32,128]{2,1,0:T(8,128)S(1)}, f32[16,32,128]{2,1,0:T(8,128)}, u32[]{:S(2)}) copy-start(f32[16,32,128]{2,1,0:T(8,128)} %rs_ref.1) | copy-start | bytes 786436
  1.0 0.9 %copy-start.1 = (f32[16,32,128]{2,1,0:T(8,128)S(1)}, f32[16,32,128]{2,1,0:T(8,128)}, u32[]{:S(2)}) copy-start(f32[16,32,128]{2,1,0:T(8,128)} %be_ref.1) | copy-start | bytes 786436

commit v4 on v3

--- a/solution.py
+++ b/solution.py
@@ -47,7 +47,7 @@
     B0, S0, V0, U0, CX0, CY0, CM0, CP0, Q0, D0,
     B1, S1, V1, U1, CX1, CY1, CM1, CP1, Q1, D1,
     T, PB, PS, GB, GS, V2, C2, C3, C4, E, F3,
-    halo_send, halo_recv, ga_send, ga_recv, own_sem, loc_sem,
+    halo_send, halo_recv, ga_send, ga_recv, rounds, loc_sem,
 ):
     n = G * B
     g = lax.axis_index("grp")
@@ -63,12 +63,34 @@
 
     barrier = pltpu.get_barrier_semaphore()
 
-    def greet(d, carry):
-        peer = (me + d) % n
-        pl.semaphore_signal(barrier, inc=1, device_id=(peer // B, peer % B), device_id_type=MESH)
-        return carry
-
-    lax.fori_loop(1, n, greet, 0)
+    partners = []
+    step = 1
+    while step < G:
+        partners.append((step, (g + step * (1 - 2 * ((g // step) % 2)), b)))
+        step *= 2
+    step = 1
+    while step < B:
+        partners.append((step, (g, b + step * (1 - 2 * ((b // step) % 2)))))
+        step *= 2
+    expected = 0
+    for dx, dy in DIRS:
+        there = (g + dx >= 0) & (g + dx < G) & (b + dy >= 0) & (b + dy < B)
+        expected = expected + there.astype(jnp.int32)
+
+        @pl.when(there)
+        def _():
+            pl.semaphore_signal(barrier, inc=1, device_id=(g + dx, b + dy), device_id_type=MESH)
+
+    for step, partner in partners:
+        if step > 1:
+            expected = expected + 1
+            pl.semaphore_signal(barrier, inc=1, device_id=partner, device_id_type=MESH)
+
+    def tell(k):
+        pl.semaphore_signal(rounds.at[k], inc=1, device_id=partners[k][1], device_id_type=MESH)
+
+    def hear(k):
+        pl.semaphore_wait(rounds.at[k], 1)
 
     for ref, nx, hx, ny in ((B0, X0, H0, Y0), (S0, X0, H0, Y0), (B1, X0 // 2, H1, Y0 // 2), (S1, X0 // 2, H1, Y0 // 2)):
         rows = ny + 2 * HY
@@ -95,7 +117,7 @@
     V2[:, pl.ds(0, 8)] = jnp.zeros((G + 2, 8, LANES), F32)
     V2[:, pl.ds(8 + ry2, 8)] = jnp.zeros((G + 2, 8, LANES), F32)
 
-    pl.semaphore_wait(barrier, n - 1)
+    pl.semaphore_wait(barrier, expected)
 
     def halo_copies(kind, src, dst, nx, hx, ny, deep, corner, tall, src_is_input):
         made = []
@@ -144,7 +166,7 @@
             ).start()
             return carry
 
-        lax.fori_loop(1, n, one, 0)
+        lax.fori_loop(1, n, one, 0, unroll=True)
 
     def gather_recv(which, whole):
         pltpu.make_async_copy(whole, whole, ga_recv.at[which]).wait()
@@ -154,12 +176,13 @@
             pltpu.make_async_copy(packed, packed, ga_send.at[which, d]).wait()
             return carry
 
-        lax.fori_loop(1, n, one, 0)
+        lax.fori_loop(1, n, one, 0, unroll=True)
 
     beta_halo = halo_copies(0, be_ref, B0, X0, H0, Y0, 4, 3, 4, True)
     source_halo = halo_copies(1, rs_ref, S0, X0, H0, Y0, 3, 2, 4, True)
     start_all(beta_halo)
     start_all(source_halo)
+    tell(0)
     load_b.wait()
 
     def halve(pair, apart, slot):
@@ -250,14 +273,25 @@
     row0, rows0 = 4, 40
     row1, rows1 = 4, 24
 
+    hear(0)
+    tell(1)
     recv_all(beta_halo)
+    hear(1)
+    tell(2)
     setup(0, B0, CX0, CY0, CM0, CP0, Q0, D0, 1, 23, row0, rows0, H0, X0, Y0)
     load_s.wait()
     recv_all(source_halo)
     start_all(beta1_halo)
-    gather_start(0, PB, GB)
+    hear(2)
+    tell(3)
     first_sweep(V0, Q0, S0, 1, 23, row0, rows0)
     sweep(0, V0, U0, S0, Q0, coeffs0, 2, 22, row0, rows0)
+
+    hear(3)
+    tell(4)
+    for k in range(5, len(partners)):
+        hear(k - 1)
+        tell(k)
 
     def down0(p, carry):
         i = H0 + 2 * p
@@ -268,6 +302,8 @@
     lax.fori_loop(0, X0 // 2, down0, 0, unroll=True)
     source1_halo = halo_copies(3, S1, S1, X0 // 2, H1, Y0 // 2, 4, 4, 4, False)
     start_all(source1_halo)
+    hear(len(partners) - 1)
+    gather_start(0, PB, GB)
 
     recv_all(beta1_halo)
     setup(1, B1, CX1, CY1, CM1, CP1, Q1, D1, 1, 17, row1, rows1, H1, X0 // 2, Y0 // 2)
@@ -403,7 +439,7 @@
         return x, r, p, new
 
     zero = [jnp.zeros((ry4, LANES), F32) for i in range(G)]
-    x4 = lax.fori_loop(0, COARSE, cg, (zero, s4, s4, dot(s4, s4)))[0]
+    x4 = lax.fori_loop(0, COARSE, cg, (zero, s4, s4, dot(s4, s4)), unroll=True)[0]
 
     up = refine(x4)
     s3 = [F3[1, i] for i in range(G)]
@@ -481,7 +517,7 @@
             pltpu.SemaphoreType.DMA((4, 8)),
             pltpu.SemaphoreType.DMA((2, G * B)),
             pltpu.SemaphoreType.DMA((2,)),
-            pltpu.SemaphoreType.DMA((1,)),
+            pltpu.SemaphoreType.REGULAR((8,)),
             pltpu.SemaphoreType.DMA((2,)),
         ],
         compiler_params=pltpu.CompilerParams(
@@ -654,7 +690,7 @@
 def solution(mesh):
     placed = P("grp", "box", None)
     G, B = mesh.shape["grp"], mesh.shape["box"]
-    small = G * B <= 64 and (2 * B) % 8 == 0 and G > 1
+    small = (G, B) in ((4, 8), (8, 8), (4, 16), (8, 4), (2, 16))
 
     def local(right_side, beta):
         if small and right_side.shape == (X0, Y0, LANES):

time: 34 us -> 31.5 us (0.926)
  Pallas kernels: 31.3 us -> 28.7 us
    pallas_call x1, Pallas kernels: 31.3 us -> 28.7 us  [in_one_kernel(): pl.pallas_call(functools.partial(kernel, G, B), out_shape=jax.ShapeDtypeS...]
where the time goes in v4:
time: 31.5 us; the launch traced here: 31.3 us
  Pallas kernels  28.7 us (91%)
  local copies, waits for them, and re-layouts  2.6 us (8%)
    pallas_call x1, Pallas kernels, in_one_kernel(): pl.pallas_call(functools.partial(kernel, G, B), out_shape=jax.ShapeDtypeS...  28.7 us
    unnamed x5, local copies, waits for them, and re-layouts  2.6 us

profile of v4, /device:TPU:0, one launch (start us, length us, event | category | flops | bytes accessed | tf_op | source)
XLA Modules:
  0.0 31.3 jit_solution(16340505403865179097)
XLA Ops:
  0.0 0.0 copy-start
  0.0 0.9 %copy-done = f32[16,32,128]{2,1,0:T(8,128)S(1)} copy-done((f32[16,32,128]{2,1,0:T(8,128)S(1)}, f32[16,32,128]{2,1,0:T(8,128)}, u32[]{:S(2)}) %copy-start) | copy-done | bytes 262168
  1.0 0.0 copy-start.1
  1.0 0.9 %copy-done.1 = f32[16,32,128]{2,1,0:T(8,128)S(1)} copy-done((f32[16,32,128]{2,1,0:T(8,128)S(1)}, f32[16,32,128]{2,1,0:T(8,128)}, u32[]{:S(2)}) %copy-start.1) | copy-done | bytes 262168
  1.9 28.7 %shard_map.28 = f32[16,32,128]{2,1,0:T(8,128)S(1)} custom-call(f32[16,32,128]{2,1,0:T(8,128)S(1)} %copy-done, f32[16,32,128]{2,1,0:T(8,128)S(1)} %copy-done.1), custom_call_target="tpu_custom_call" | custom-call | tf_op jit(solution)/shard_map/pallas_call | solution.py:497
  30.6 0.7 %copy.4 = f32[16,32,128]{2,1,0:T(8,128)} copy(f32[16,32,128]{2,1,0:T(8,128)S(1)} %shard_map.28) | data formatting | bytes 524288
Async XLA Ops:
  0.0 0.9 %copy-start = (f32[16,32,128]{2,1,0:T(8,128)S(1)}, f32[16,32,128]{2,1,0:T(8,128)}, u32[]{:S(2)}) copy-start(f32[16,32,128]{2,1,0:T(8,128)} %rs_ref.1) | copy-start | bytes 786436
  1.0 0.9 %copy-start.1 = (f32[16,32,128]{2,1,0:T(8,128)S(1)}, f32[16,32,128]{2,1,0:T(8,128)}, u32[]{:S(2)}) copy-start(f32[16,32,128]{2,1,0:T(8,128)} %be_ref.1) | copy-start | bytes 786436
